TPU v7x, 32 devices: a whole 2x2x4 slice. The times are simulated.
32 devices in a mesh: grp: 2 (over y), train: 4 (over z), test: 4 (over x, core).
Axes of the slice: x: 2, y: 2, z: 4, core: 2. Of those that a mesh axis runs over, the one named last changes fastest.
Arguments:
- test_features: bfloat16 [512, 16384], P('test', 'train'), may hold values from -6 to 6
- inverse_kernel: bfloat16 [16384, 16384], P('train', 'test'), may hold values from -0.046875 to 0.046875
- train_features: bfloat16 [2048, 16384], P(('grp', 'train'), 'test'), parts along dimension 0, may hold values from -0.046875 to 0.046875
Outputs:
- scores: float32 [512, 2048], P('test', ('grp', 'train')), parts along dimension 1
There are 2 independent parts, one for each index of `grp`. A program takes and returns all parts, laid end to end along the dimension named above; an argument that names none is the same for every part. Nothing has to cross between parts.
All inputs are finite; a program needn't handle non-finite values.
Results may differ from a plain program's by a relative error of at most 0.0029.
Values may be sent and summed in bfloat16 or wider, within the bound.
A program may use at most 128 MiB of HBM per device.

v0:
```python
import jax
import jax.numpy as jnp
from jax import lax
from jax.sharding import PartitionSpec as P


def on_device(test_features, inverse_kernel, train_features):
    gathered = lax.all_gather(test_features, "test", axis=0, tiled=True)
    partial_value = jnp.dot(gathered, inverse_kernel, preferred_element_type=jnp.float32)
    conditioned = lax.psum(partial_value, "train").astype(jnp.bfloat16)
    partial_scores = lax.dot_general(
        conditioned, train_features, (((1,), (1,)), ((), ())), preferred_element_type=jnp.float32
    )
    return lax.psum_scatter(partial_scores, "test", scatter_dimension=0, tiled=True)


def solution(mesh):
    return jax.shard_map(
        on_device,
        mesh=mesh,
        in_specs=(P("test", "train"), P("train", "test"), P(("grp", "train"), "test")),
        out_specs=P("test", ("grp", "train")),
        check_vma=False,
    )
```

profile of v0, /device:TPU:1, one launch (start us, length us, event | category | flops | bytes accessed | tf_op | source)
XLA Modules:
  0.0 387.3 jit_solution(13621107759392685735)
XLA Ops:
  6.5 0.0 copy-start
  6.5 0.0 all-gather.2.cloned.1.call-start
  6.5 0.7 all-gather.2.cloned.1.call-update
  7.3 0.0 reduce-scatter.2.cloned.1.call-start
  7.3 38.6 %all-gather.2.cloned.1.call-done = bf16[512,4096]{1,0:T(8,128)(2,1)} async-done(((bf16[128,4096]{1,0:T(8,128)(2,1)}), bf16[512,4096]{1,0:T(8,128)(2,1)}) %all-gather.2.cloned.1.call-update) | async-done | bytes 4194320 | tf_op jit(solution)/shard_map/all_gather | solution.py:8
  45.9 23.9 %fusion.2 = f32[512,4096]{1,0:T(8,128)} fusion(bf16[512,4096]{1,0:T(8,128)(2,1)} %all-gather.2.cloned.1.call-done, bf16[4096,4096]{1,0:T(8,128)(2,1)} %param.4), kind=kOutput, calls=%fused_computation.2 | convolution fusion | flops 17179869184 | bytes 46137344 | tf_op jit(solution)/shard_map/dot_general | solution.py:9
  69.8 284.8 %all-reduce.1 = bf16[512,4096]{1,0:T(8,128)(2,1)} all-reduce(f32[512,4096]{1,0:T(8,128)} %fusion.2), channel_id=1, replica_groups=mesh['grp'=2,'train'=4,'test'=4] {'train'}, use_global_device_ids=true, to_apply=%region_0.0 | all-reduce | flops 2097152 | bytes 12582912 | tf_op jit(solution)/shard_map/psum | solution.py:10
  354.6 0.0 copy-done
  354.6 4.2 %fusion.3 = f32[512,256]{1,0:T(8,128)} fusion(bf16[512,4096]{1,0:T(8,128)(2,1)} %all-reduce.1, bf16[256,4096]{1,0:T(8,128)(2,1)S(1)} %copy-done), kind=kOutput, calls=%fused_computation.3 | convolution fusion | flops 1073741824 | bytes 6815744 | tf_op jit(solution)/shard_map/dot_general | solution.py:11
  358.8 0.0 reduce-scatter.2.cloned.1.call-update
  358.9 21.6 %reduce-scatter.2.cloned.1.call-done = f32[128,256]{1,0:T(8,128)} async-done(((f32[512,256]{1,0:T(8,128)}), f32[128,256]{1,0:T(8,128)}) %reduce-scatter.2.cloned.1.call-update) | async-done | bytes 131088 | tf_op jit(solution)/shard_map/reduce_scatter | solution.py:14
Async XLA Ops:
  6.5 348.1 %copy-start = (bf16[256,4096]{1,0:T(8,128)(2,1)S(1)}, bf16[256,4096]{1,0:T(8,128)(2,1)}, u32[]{:S(2)}) copy-start(bf16[256,4096]{1,0:T(8,128)(2,1)} %param.5) | copy-start | bytes 6291460
  6.5 39.4 %all-gather.2.cloned.1.call-start = ((), (), s32[]{:S(2)}) async-start(), calls=%async_computation.1 | async-start | bytes 5242880 | tf_op jit(solution)/shard_map/all_gather | solution.py:8
  7.3 373.2 %reduce-scatter.2.cloned.1.call-start = ((), (), s32[]{:S(2)}) async-start(), calls=%async_computation.2 | async-start | bytes 655360 | tf_op jit(solution)/shard_map/reduce_scatter | solution.py:14
Sparse Core Ops, SparseCore 0:
  8.9 36.9 all-gather.1
  359.0 21.4 reduce-scatter.1
where the time goes:
time: 388 us; the launch traced here: 387 us
  blocking collectives  285 us (73%)
  waiting for transfers between devices  60.9 us (16%)
  matrix products  28.1 us (7%)
  between operations  13.4 us (3%)
    psum x1, blocking collectives, on_device(): conditioned = lax.psum(partial_value, 'train').astype(jnp.bfloat16)  285 us
    all_gather x1, waiting for transfers between devices, on_device(): gathered = lax.all_gather(test_features, 'test', axis=0, tiled=True)  38.6 us
    dot_general x1, matrix products, on_device(): jnp.dot(gathered, inverse_kernel, preferred_element_type=jnp.float32)  23.9 us
    reduce_scatter x1, waiting for transfers between devices, on_device(): lax.psum_scatter(partial_scores, 'test', scatter_dimension=0, tiled=True)  21.6 us
  transfers between devices with their start and end apart: 2, of which 2 were waited for; matrix products, arithmetic and copies ran while one was open for 0% of the time, Pallas kernels for 0%

commit v1 on v0

v1 whole, which is shorter than its diff:
```python
import functools

import jax
import jax.numpy as jnp
from jax import lax
from jax.experimental import pallas as pl
from jax.experimental.pallas import tpu as pltpu
from jax.sharding import PartitionSpec as P

CORES = 2
WIDTH = 256
SKEW = 2
MESH = pl.DeviceIdType.MESH


def kernel(
    n_grp, n_train, n_test, width, skew,
    test_hbm, kernel_hbm, train_hbm, out_ref,
    test_v, kernel_v, train_v, part, arrived, cond, acc, acc_in,
    kernel_sem, train_sem, own_sem,
    test_send, test_recv, pair_send, pair_recv,
    sum_send, sum_recv, total_send, total_recv, grp_send, grp_recv,
    score_send, score_recv,
):
    grp, z, me = lax.axis_index("grp"), lax.axis_index("train"), lax.axis_index("test")
    nx = n_test // CORES
    x, core = me // CORES, lax.rem(me, CORES)
    half = test_hbm.shape[0] // n_grp
    block = CORES * half
    per_pass = kernel_hbm.shape[1] // (2 * width)
    chunks = nx * per_pass
    last = n_train - 1

    def device(h, c):
        return lax.rem(x + h + nx, nx) * CORES + c

    def columns(way, j):
        return pl.ds(pl.multiple_of((way * per_pass + j) * width, width), width)

    def kernel_copy(way, j):
        slot = way * per_pass + j
        return pltpu.make_async_copy(kernel_hbm.at[:, columns(way, j)], kernel_v.at[slot], kernel_sem.at[slot])

    train_copy = pltpu.make_async_copy(train_hbm, train_v, train_sem)
    own_rows = test_hbm.at[pl.ds(pl.multiple_of(grp * half, half), half)]
    own_slot = pl.ds(pl.multiple_of(core * half, half), half)
    own_copy = pltpu.make_async_copy(own_rows, test_v.at[0, own_slot], own_sem)

    own_copy.start()
    for j in range(min(2, per_pass)):
        for way in range(2):
            kernel_copy(way, j).start()
    train_copy.start()

    barrier = pltpu.get_barrier_semaphore()
    for step in range(1, n_test):
        pl.semaphore_signal(barrier, inc=1, device_id={"test": lax.rem(me + step, n_test)}, device_id_type=MESH)
    for step in range(1, n_grp):
        pl.semaphore_signal(barrier, inc=1, device_id={"grp": lax.rem(grp + step, n_grp)}, device_id_type=MESH)

    @pl.when(z > 0)
    def _():
        pl.semaphore_signal(barrier, inc=1, device_id={"train": z - 1}, device_id_type=MESH)

    @pl.when(z < last)
    def _():
        pl.semaphore_signal(barrier, inc=1, device_id={"train": z + 1}, device_id_type=MESH)

    acc[...] = jnp.zeros_like(acc)
    near = jnp.where(z > 0, 1, 0) + jnp.where(z < last, 1, 0)
    pl.semaphore_wait(barrier, n_test - 1 + n_grp - 1 + near)

    def test_copy(h):
        return pltpu.make_async_remote_copy(
            src_ref=own_rows, dst_ref=test_v.at[h, own_slot],
            send_sem=test_send.at[h], recv_sem=test_recv.at[h],
            device_id={"test": device(-h, core)}, device_id_type=MESH,
        )

    def pair_copy(h):
        return pltpu.make_async_remote_copy(
            src_ref=own_rows if h == 0 else test_v.at[h, own_slot], dst_ref=test_v.at[h, own_slot],
            send_sem=pair_send.at[h], recv_sem=pair_recv.at[h],
            device_id={"test": device(0, 1 - core)}, device_id_type=MESH,
        )

    pair_copy(0).start()
    for h in range(1, nx):
        test_copy(h).start()
    own_copy.wait()
    pair_copy(0).wait_recv()

    def sum_copy(way, q):
        return pltpu.make_async_remote_copy(
            src_ref=part.at[way, q], dst_ref=arrived.at[way, q],
            send_sem=sum_send.at[way, q], recv_sem=sum_recv.at[way, q],
            device_id={"train": jnp.minimum(z + 1, last) if way == 0 else jnp.maximum(z - 1, 0)},
            device_id_type=MESH,
        )

    my_rows = pl.ds(pl.multiple_of(grp * block, block), block)

    def total_copy(way, q):
        ref = cond.at[way, q, my_rows]
        return pltpu.make_async_remote_copy(
            src_ref=ref, dst_ref=ref,
            send_sem=total_send.at[way, q], recv_sem=total_recv.at[way, q],
            device_id={"train": jnp.maximum(z - 1, 0) if way == 0 else jnp.minimum(z + 1, last)},
            device_id_type=MESH,
        )

    def grp_copy(way, q, step):
        ref = cond.at[way, q, my_rows]
        return pltpu.make_async_remote_copy(
            src_ref=ref, dst_ref=ref,
            send_sem=grp_send.at[way, q, step], recv_sem=grp_recv.at[way, q, step],
            device_id={"grp": lax.rem(grp + step, n_grp)}, device_id_type=MESH,
        )

    def inside(q):
        return (q >= 0) & (q < chunks)

    def do_step(s, carry):
        for way in range(2):
            @pl.when(s + 2 < per_pass)
            def _():
                kernel_copy(way, s + 2).start()

        @pl.when(s == 1)
        def _():
            train_copy.wait()

        for h in range(1, nx):
            @pl.when(s == h * per_pass + skew * jnp.minimum(z, last - z))
            def _():
                test_copy(h).wait_recv()
                pair_copy(h).start()
                pair_copy(h).wait_recv()

        for way in range(2):
            place = z if way == 0 else last - z
            q = s - skew * place

            @pl.when(inside(q))
            def _():
                h, j = q // per_pass, lax.rem(q, per_pass)

                @pl.when(q < per_pass)
                def _():
                    kernel_copy(way, j).wait()

                part[way, q] = jnp.dot(
                    test_v[h], kernel_v[way * per_pass + j], preferred_element_type=jnp.float32
                )

        for way in range(2):
            place = z if way == 0 else last - z
            q = s - skew * place

            @pl.when(inside(q) & (place > 0))
            def _():
                sum_copy(way, q).wait_recv()
                part[way, q] += arrived[way, q]

            @pl.when(inside(q) & (place < last))
            def _():
                sum_copy(way, q).start()

            @pl.when(inside(q) & (place == last))
            def _():
                cond[way, q, my_rows] = part[way, q].astype(jnp.bfloat16)

        for way in range(2):
            place = z if way == 0 else last - z
            q = s - skew * (2 * last - place)

            @pl.when(inside(q) & (place < last))
            def _():
                total_copy(way, q).wait_recv()

            @pl.when(inside(q) & (place > 0))
            def _():
                total_copy(way, q).start()

            @pl.when(inside(q))
            def _():
                for step in range(1, n_grp):
                    grp_copy(way, q, step).start()

        for way in range(2):
            place = z if way == 0 else last - z
            q = s - skew * (2 * last - place) - skew

            @pl.when(inside(q))
            def _():
                h, j = q // per_pass, lax.rem(q, per_pass)
                for step in range(1, n_grp):
                    grp_copy(way, q, step).wait_recv()
                value = lax.dot_general(
                    cond[way, q], train_v[:, columns(way, j)],
                    (((1,), (1,)), ((), ())), preferred_element_type=jnp.float32,
                )
                for c in range(CORES):
                    for g in range(n_grp):
                        begin = g * block + c * half
                        acc[h, c, g] += value[begin:begin + half]

        return carry

    lax.fori_loop(0, chunks + skew * (2 * last + 1), do_step, 0)

    def score_copy(h, flip):
        c = lax.rem(core + flip, CORES)
        return pltpu.make_async_remote_copy(
            src_ref=acc.at[h, c], dst_ref=acc_in.at[h, flip],
            send_sem=score_send.at[h, flip], recv_sem=score_recv.at[h, flip],
            device_id={"test": device(h, c)}, device_id_type=MESH,
        )

    others = [(h, flip) for h in range(nx - 1, -1, -1) for flip in range(CORES) if (h, flip) != (0, 0)]
    for h, flip in others:
        score_copy(h, flip).start()

    pair_copy(0).wait_send()
    for h in range(1, nx):
        test_copy(h).wait_send()
        pair_copy(h).wait_send()

    def drain(q, carry):
        for way in range(2):
            place = z if way == 0 else last - z

            @pl.when(place < last)
            def _():
                sum_copy(way, q).wait_send()

            @pl.when(place > 0)
            def _():
                total_copy(way, q).wait_send()

            for step in range(1, n_grp):
                grp_copy(way, q, step).wait_send()
        return carry

    lax.fori_loop(0, chunks, drain, 0)

    for h, flip in reversed(others):
        score_copy(h, flip).wait_recv()
    for g in range(n_grp):
        value = acc[0, core, g]
        for h, flip in others:
            value = value + acc_in[h, flip, g]
        out_ref[g * half:(g + 1) * half] = value
    for h, flip in others:
        score_copy(h, flip).wait_send()


def on_device(sizes, test_features, inverse_kernel, train_features):
    n_grp, n_train, n_test = sizes
    nx = n_test // CORES
    rows, depth = test_features.shape
    half = rows // n_grp
    block = CORES * half
    width = min(WIDTH, inverse_kernel.shape[1] // 2)
    per_pass = inverse_kernel.shape[1] // (2 * width)
    chunks = nx * per_pass
    trains = train_features.shape[0]
    dma = pltpu.SemaphoreType.DMA
    return pl.pallas_call(
        functools.partial(kernel, n_grp, n_train, n_test, width, SKEW),
        out_shape=jax.ShapeDtypeStruct((rows, trains), jnp.float32),
        in_specs=[pl.BlockSpec(memory_space=pl.ANY)] * 3,
        out_specs=pl.BlockSpec(memory_space=pltpu.VMEM),
        scratch_shapes=[
            pltpu.VMEM((nx, block, depth), jnp.bfloat16),
            pltpu.VMEM((2 * per_pass, depth, width), jnp.bfloat16),
            pltpu.VMEM(train_features.shape, jnp.bfloat16),
            pltpu.VMEM((2, chunks, block, width), jnp.float32),
            pltpu.VMEM((2, chunks, block, width), jnp.float32),
            pltpu.VMEM((2, chunks, n_grp * block, width), jnp.bfloat16),
            pltpu.VMEM((nx, CORES, n_grp, half, trains), jnp.float32),
            pltpu.VMEM((nx, CORES, n_grp, half, trains), jnp.float32),
            dma((2 * per_pass,)), dma, dma,
            dma((nx,)), dma((nx,)), dma((nx,)), dma((nx,)),
            dma((2, chunks)), dma((2, chunks)),
            dma((2, chunks)), dma((2, chunks)),
            dma((2, chunks, n_grp)), dma((2, chunks, n_grp)),
            dma((nx, CORES)), dma((nx, CORES)),
        ],
        compiler_params=pltpu.CompilerParams(
            collective_id=0, has_side_effects=True, vmem_limit_bytes=60 * 1024 * 1024
        ),
        cost_estimate=pl.CostEstimate(
            flops=2 * nx * block * depth * inverse_kernel.shape[1],
            bytes_accessed=2 * depth * inverse_kernel.shape[1], transcendentals=0,
        ),
    )(test_features, inverse_kernel, train_features)


def solution(mesh):
    sizes = tuple(mesh.shape[axis] for axis in ("grp", "train", "test"))
    return jax.shard_map(
        functools.partial(on_device, sizes),
        mesh=mesh,
        in_specs=(P("test", "train"), P("train", "test"), P(("grp", "train"), "test")),
        out_specs=P("test", ("grp", "train")),
        check_vma=False,
    )
```

time: 388 us -> 106 us (0.27)
  blocking collectives: 285 us -> 0 us
  Pallas kernels: 0 us -> 104 us
  waiting for transfers between devices: 60.9 us -> 0 us
  matrix products: 28.1 us -> 0 us
  between operations: 13.4 us -> 0.01 us
    psum x1 -> x0, blocking collectives: 285 us -> none  [on_device(): conditioned = lax.psum(partial_value, 'train').astype(jnp.bfloat16)]
    pallas_call x0 -> x1, Pallas kernels: none -> 104 us  [on_device(): pl.pallas_call(functools.partial(kernel, n_grp, n_train, n_test, width, S...]
    all_gather x1 -> x0, waiting for transfers between devices: 38.6 us -> none  [on_device(): gathered = lax.all_gather(test_features, 'test', axis=0, tiled=True)]
    dot_general x2 -> x0, matrix products: 28.1 us -> none  [the longest x1 23.9 us: on_device(): jnp.dot(gathered, inverse_kernel, preferred_element_type=jnp.float32)]
    reduce_scatter x1 -> x0, waiting for transfers between devices: 21.6 us -> none  [on_device(): lax.psum_scatter(partial_scores, 'test', scatter_dimension=0, tiled=True)]
  transfers between devices with their start and end apart: 2 -> 0, of which waited for: 2 -> 0; matrix products, arithmetic and copies ran while one was open for 0% -> 0% of each run, Pallas kernels for 0% -> 0%
where the time goes in v1:
time: 106 us
  Pallas kernels  104 us (98%)
  local copies, waits for them, and re-layouts  1.57 us (1%)
    pallas_call x1, Pallas kernels, on_device(): pl.pallas_call(functools.partial(kernel, n_grp, n_train, n_test, width, S...  104 us

profile of v1, /device:TPU:1, one launch (start us, length us, event | category | flops | bytes accessed | tf_op | source)
XLA Modules:
  0.0 105.7 jit_solution(17526218389376583542)
XLA Ops:
  0.0 104.1 %shard_map.37 = f32[128,256]{1,0:T(8,128)} custom-call(bf16[128,4096]{1,0:T(8,128)(2,1)} %test_hbm.1, bf16[4096,4096]{1,0:T(8,128)(2,1)} %kernel_hbm.1, bf16[256,4096]{1,0:T(8,128)(2,1)} %train_hbm.1), custom_call_target="tpu_custom_call" | custom-call | flops 8589934592 | bytes 33554432 | tf_op jit(solution)/shard_map/pallas_call | solution.py:269
  104.1 1.6 %copy.5 = f32[128,256]{1,0:T(8,128)} copy(f32[128,256]{1,0:T(8,128)} %shard_map.37) | data formatting | bytes 262144

commit v2 on v1

--- a/solution.py
+++ b/solution.py
@@ -30,6 +30,16 @@
     per_pass = kernel_hbm.shape[1] // (2 * width)
     chunks = nx * per_pass
     last = n_train - 1
+    lead = max(1, per_pass // 2)
+    middle = lead + (nx - 1) * per_pass
+
+    def split(q):
+        other = q - lead
+        own = (q < lead) | (q >= middle)
+        h = jnp.where(own, 0, 1 + other // per_pass)
+        j = jnp.where(q < lead, q, jnp.where(own, other - (nx - 1) * per_pass + lead, lax.rem(other + per_pass, per_pass)))
+        first = (q < lead) | ((h <= 1) & (q < lead + per_pass) & (j >= lead))
+        return h, j, first
 
     def device(h, c):
         return lax.rem(x + h + nx, nx) * CORES + c
@@ -50,7 +60,6 @@
     for j in range(min(2, per_pass)):
         for way in range(2):
             kernel_copy(way, j).start()
-    train_copy.start()
 
     barrier = pltpu.get_barrier_semaphore()
     for step in range(1, n_test):
@@ -120,6 +129,17 @@
     def inside(q):
         return (q >= 0) & (q < chunks)
 
+    def score_copy(h, flip):
+        c = lax.rem(core + flip, CORES)
+        return pltpu.make_async_remote_copy(
+            src_ref=acc.at[h, c], dst_ref=acc_in.at[h, flip],
+            send_sem=score_send.at[h, flip], recv_sem=score_recv.at[h, flip],
+            device_id={"test": device(h, c)}, device_id_type=MESH,
+        )
+
+    far = [(h, flip) for h in range(1, nx) for flip in range(CORES)]
+    others = far + [(0, 1)]
+
     def do_step(s, carry):
         for way in range(2):
             @pl.when(s + 2 < per_pass)
@@ -128,10 +148,14 @@
 
         @pl.when(s == 1)
         def _():
+            train_copy.start()
+
+        @pl.when(s == 2 * skew)
+        def _():
             train_copy.wait()
 
         for h in range(1, nx):
-            @pl.when(s == h * per_pass + skew * jnp.minimum(z, last - z))
+            @pl.when(s == lead + (h - 1) * per_pass + skew * jnp.minimum(z, last - z))
             def _():
                 test_copy(h).wait_recv()
                 pair_copy(h).start()
@@ -143,9 +167,9 @@
 
             @pl.when(inside(q))
             def _():
-                h, j = q // per_pass, lax.rem(q, per_pass)
-
-                @pl.when(q < per_pass)
+                h, j, first = split(q)
+
+                @pl.when(first)
                 def _():
                     kernel_copy(way, j).wait()
 
@@ -193,7 +217,7 @@
 
             @pl.when(inside(q))
             def _():
-                h, j = q // per_pass, lax.rem(q, per_pass)
+                h, j, _ = split(q)
                 for step in range(1, n_grp):
                     grp_copy(way, q, step).wait_recv()
                 value = lax.dot_general(
@@ -205,21 +229,15 @@
                         begin = g * block + c * half
                         acc[h, c, g] += value[begin:begin + half]
 
+        @pl.when(s == middle - 1 + skew * (jnp.maximum(2 * last - z, last + z) + 1))
+        def _():
+            for h, flip in far:
+                score_copy(h, flip).start()
+
         return carry
 
     lax.fori_loop(0, chunks + skew * (2 * last + 1), do_step, 0)
-
-    def score_copy(h, flip):
-        c = lax.rem(core + flip, CORES)
-        return pltpu.make_async_remote_copy(
-            src_ref=acc.at[h, c], dst_ref=acc_in.at[h, flip],
-            send_sem=score_send.at[h, flip], recv_sem=score_recv.at[h, flip],
-            device_id={"test": device(h, c)}, device_id_type=MESH,
-        )
-
-    others = [(h, flip) for h in range(nx - 1, -1, -1) for flip in range(CORES) if (h, flip) != (0, 0)]
-    for h, flip in others:
-        score_copy(h, flip).start()
+    score_copy(0, 1).start()
 
     pair_copy(0).wait_send()
     for h in range(1, nx):
@@ -244,7 +262,7 @@
 
     lax.fori_loop(0, chunks, drain, 0)
 
-    for h, flip in reversed(others):
+    for h, flip in others:
         score_copy(h, flip).wait_recv()
     for g in range(n_grp):
         value = acc[0, core, g]

time: 106 us -> 101 us (0.953)
  Pallas kernels: 104 us -> 99.7 us
    pallas_call x1, Pallas kernels: 104 us -> 99.7 us  [on_device(): pl.pallas_call(functools.partial(kernel, n_grp, n_train, n_test, width, S...]
where the time goes in v2:
time: 101 us
  Pallas kernels  99.7 us (99%)
  local copies, waits for them, and re-layouts  1.57 us (2%)
    pallas_call x1, Pallas kernels, on_device(): pl.pallas_call(functools.partial(kernel, n_grp, n_train, n_test, width, S...  99.7 us

profile of v2, /device:TPU:1, one launch (start us, length us, event | category | flops | bytes accessed | tf_op | source)
XLA Modules:
  0.0 101.3 jit_solution(7749560531350542893)
XLA Ops:
  0.0 99.7 %shard_map.37 = f32[128,256]{1,0:T(8,128)} custom-call(bf16[128,4096]{1,0:T(8,128)(2,1)} %test_hbm.1, bf16[4096,4096]{1,0:T(8,128)(2,1)} %kernel_hbm.1, bf16[256,4096]{1,0:T(8,128)(2,1)} %train_hbm.1), custom_call_target="tpu_custom_call" | custom-call | flops 8589934592 | bytes 33554432 | tf_op jit(solution)/shard_map/pallas_call | solution.py:287
  99.7 1.6 %copy.5 = f32[128,256]{1,0:T(8,128)} copy(f32[128,256]{1,0:T(8,128)} %shard_map.37) | data formatting | bytes 262144

commit v3 on v2

--- a/solution.py
+++ b/solution.py
@@ -10,6 +10,8 @@
 CORES = 2
 WIDTH = 256
 SKEW = 2
+BACK = 2
+SIDE = 4
 MESH = pl.DeviceIdType.MESH
 
 
@@ -196,7 +198,7 @@
 
         for way in range(2):
             place = z if way == 0 else last - z
-            q = s - skew * (2 * last - place)
+            q = s - skew * last - BACK * (last - place)
 
             @pl.when(inside(q) & (place < last))
             def _():
@@ -213,7 +215,7 @@
 
         for way in range(2):
             place = z if way == 0 else last - z
-            q = s - skew * (2 * last - place) - skew
+            q = s - skew * last - BACK * (last - place) - SIDE
 
             @pl.when(inside(q))
             def _():
@@ -229,14 +231,14 @@
                         begin = g * block + c * half
                         acc[h, c, g] += value[begin:begin + half]
 
-        @pl.when(s == middle - 1 + skew * (jnp.maximum(2 * last - z, last + z) + 1))
+        @pl.when(s == middle - 1 + skew * last + BACK * jnp.maximum(last - z, z) + SIDE)
         def _():
             for h, flip in far:
                 score_copy(h, flip).start()
 
         return carry
 
-    lax.fori_loop(0, chunks + skew * (2 * last + 1), do_step, 0)
+    lax.fori_loop(0, chunks + (skew + BACK) * last + SIDE, do_step, 0)
     score_copy(0, 1).start()
 
     pair_copy(0).wait_send()

time: 101 us -> 101 us (level)
  no operation moved by 1% of the time
where the time goes in v3:
time: 101 us
  Pallas kernels  99.7 us (99%)
  local copies, waits for them, and re-layouts  1.57 us (2%)
    pallas_call x1, Pallas kernels, on_device(): pl.pallas_call(functools.partial(kernel, n_grp, n_train, n_test, width, S...  99.7 us

profile of v3, /device:TPU:1, one launch (start us, length us, event | category | flops | bytes accessed | tf_op | source)
XLA Modules:
  0.0 101.3 jit_solution(8957079914350318537)
XLA Ops:
  0.0 99.7 %shard_map.37 = f32[128,256]{1,0:T(8,128)} custom-call(bf16[128,4096]{1,0:T(8,128)(2,1)} %test_hbm.1, bf16[4096,4096]{1,0:T(8,128)(2,1)} %kernel_hbm.1, bf16[256,4096]{1,0:T(8,128)(2,1)} %train_hbm.1), custom_call_target="tpu_custom_call" | custom-call | flops 8589934592 | bytes 33554432 | tf_op jit(solution)/shard_map/pallas_call | solution.py:289
  99.7 1.6 %copy.5 = f32[128,256]{1,0:T(8,128)} copy(f32[128,256]{1,0:T(8,128)} %shard_map.37) | data formatting | bytes 262144

commit v4 on v3

--- a/solution.py
+++ b/solution.py
@@ -32,7 +32,7 @@
     per_pass = kernel_hbm.shape[1] // (2 * width)
     chunks = nx * per_pass
     last = n_train - 1
-    lead = max(1, per_pass // 2)
+    lead = max(1, 5 * per_pass // 8)
     middle = lead + (nx - 1) * per_pass
 
     def split(q):

time: 101 us -> 100 us (0.990)
  no operation moved by 1% of the time
where the time goes in v4:
time: 100 us
  Pallas kernels  98.8 us (99%)
  local copies, waits for them, and re-layouts  1.57 us (2%)
    pallas_call x1, Pallas kernels, on_device(): pl.pallas_call(functools.partial(kernel, n_grp, n_train, n_test, width, S...  98.8 us

profile of v4, /device:TPU:1, one launch (start us, length us, event | category | flops | bytes accessed | tf_op | source)
XLA Modules:
  0.0 100.3 jit_solution(16573763215361790403)
XLA Ops:
  0.0 98.8 %shard_map.37 = f32[128,256]{1,0:T(8,128)} custom-call(bf16[128,4096]{1,0:T(8,128)(2,1)} %test_hbm.1, bf16[4096,4096]{1,0:T(8,128)(2,1)} %kernel_hbm.1, bf16[256,4096]{1,0:T(8,128)(2,1)} %train_hbm.1), custom_call_target="tpu_custom_call" | custom-call | flops 8589934592 | bytes 33554432 | tf_op jit(solution)/shard_map/pallas_call | solution.py:289
  98.8 1.6 %copy.5 = f32[128,256]{1,0:T(8,128)} copy(f32[128,256]{1,0:T(8,128)} %shard_map.37) | data formatting | bytes 262144
